TPU v7x, 256 devices: a whole 4x4x8 slice. The times are simulated.
256 devices in a mesh: rep: 8 (over z_lo, y), fsdp: 32 (over z_hi, x, core).
Axes of the slice: x: 4, y: 4, z: 8 (z_hi: 4, z_lo: 2; z = z_hi * 2 + z_lo), core: 2. Of those that a mesh axis runs over, the one named last changes fastest.
Arguments:
- activations: bfloat16 [131072, 4096], P(('rep', 'fsdp')), may hold values from -6 to 6
- norm_gain: float32 [8, 4096], P('rep', 'fsdp'), may hold values from 0.5 to 1.5
- key_weight: float32 [8, 4096, 512], P('rep', 'fsdp'), may hold values from -6 to 6
- value_weight: float32 [8, 4096, 512], P('rep', 'fsdp'), may hold values from -6 to 6
- key_cotangent: bfloat16 [131072, 512], P(('rep', 'fsdp')), may hold values from -6 to 6
- value_cotangent: bfloat16 [131072, 512], P(('rep', 'fsdp')), may hold values from -6 to 6
- step_index: int32 [1], replicated, may hold values from 0 to 63
- plan: int32 [8], replicated, may hold values from 0 to 7, as said below
Outputs:
- keys: bfloat16 [131072, 512], P(('rep', 'fsdp'))
- values: bfloat16 [131072, 512], P(('rep', 'fsdp'))
- input_grad: bfloat16 [131072, 4096], P(('rep', 'fsdp'))
- new_key_weight: float32 [8, 4096, 512], P('rep', 'fsdp')
- new_value_weight: float32 [8, 4096, 512], P('rep', 'fsdp')
- new_gain: float32 [8, 4096], P('rep', 'fsdp')
Inputs may be any that keep to these rules, and one draw needn't show every extreme that they name: `plan`: each entry is a partner mask, 0 meaning no partner; every value from 0 to 7 appears.
All inputs are finite; a program needn't handle non-finite values.
Results may differ from a plain program's by a relative error of at most 0.0095.
Values may be sent and summed in bfloat16 or wider, within the bound.
A program may use at most 128 MiB of HBM per device.

v0:
```python
import math

import jax
import jax.numpy as jnp
from jax import lax
from jax.sharding import PartitionSpec as P

lr_weight = 0.25
lr_gain = 0.005


def for_sending(shard):
    return jax.tree.map(lambda a: a.astype(jnp.bfloat16) if a.dtype == jnp.float32 else a, shard)


def swapped(shard, axis, apart):
    return lax.ppermute(shard, axis, [(i, i ^ 1 << apart) for i in range(lax.axis_size(axis))])


def body(
    activations,
    norm_gain,
    key_weight,
    value_weight,
    key_cotangent,
    value_cotangent,
    step_index,
    plan,
):
    width = activations.shape[1]
    root_inv = 1.0 / math.sqrt(width)
    bit_total = lax.axis_size("rep").bit_length() - 1
    hop_mask = plan[step_index[0] % plan.shape[0]]
    own_params = (key_weight[0], value_weight[0], norm_gain[0])
    widened = activations.astype(jnp.float32)
    inv_rms = lax.rsqrt(jnp.mean(widened * widened, axis=-1, keepdims=True) + 1e-05)
    normed = widened * inv_rms
    key_b = key_weight[0].astype(jnp.bfloat16)
    value_b = value_weight[0].astype(jnp.bfloat16)
    gain_b = norm_gain[0].astype(jnp.bfloat16)
    key_piece = lax.all_gather(key_b, "fsdp", axis=0, tiled=True)
    value_piece = lax.all_gather(value_b, "fsdp", axis=0, tiled=True)
    gain_piece = lax.all_gather(gain_b, "fsdp", axis=0, tiled=True)
    columns = (normed * gain_piece).astype(jnp.bfloat16)
    key_acc = jnp.dot(columns, key_piece, preferred_element_type=jnp.float32)
    value_acc = jnp.dot(columns, value_piece, preferred_element_type=jnp.float32)
    key_piece, value_piece = lax.all_gather((key_b, value_b), "fsdp", axis=0, tiled=True)
    dnormed_in = (
        lax.dot_general(
            key_cotangent, key_piece, (((1,), (1,)), ((), ())), preferred_element_type=jnp.float32
        )
        + lax.dot_general(
            value_cotangent,
            value_piece,
            (((1,), (1,)), ((), ())),
            preferred_element_type=jnp.float32,
        )
    ) * root_inv
    keys = (key_acc * root_inv).astype(jnp.bfloat16)
    values = (value_acc * root_inv).astype(jnp.bfloat16)
    dnormed = dnormed_in * gain_piece
    inner = jnp.mean(dnormed * normed, axis=-1, keepdims=True)
    input_grad = (inv_rms * (dnormed - normed * inner)).astype(jnp.bfloat16)
    key_term = (
        lax.dot_general(
            columns, key_cotangent, (((0,), (0,)), ((), ())), preferred_element_type=jnp.float32
        )
        * root_inv
    )
    value_term = (
        lax.dot_general(
            columns, value_cotangent, (((0,), (0,)), ((), ())), preferred_element_type=jnp.float32
        )
        * root_inv
    )
    gain_term = jnp.sum(dnormed_in * normed, axis=0)
    key_grad, value_grad, gain_grad = (
        lax.psum_scatter(
            key_term.astype(jnp.bfloat16), "fsdp", scatter_dimension=0, tiled=True
        ).astype(jnp.float32),
        lax.psum_scatter(
            value_term.astype(jnp.bfloat16), "fsdp", scatter_dimension=0, tiled=True
        ).astype(jnp.float32),
        lax.psum_scatter(
            gain_term.astype(jnp.bfloat16), "fsdp", scatter_dimension=0, tiled=True
        ).astype(jnp.float32),
    )
    own_new = (
        own_params[0] - lr_weight * key_grad,
        own_params[1] - lr_weight * value_grad,
        own_params[2] - lr_gain * gain_grad,
    )
    partner_new = own_new
    for bit_pos in range(bit_total):
        arrived = swapped(
            (for_sending(partner_new[0]), for_sending(partner_new[1]), for_sending(partner_new[2])),
            "rep",
            bit_pos,
        )
        use_bit = jnp.right_shift(hop_mask, bit_pos) % 2 == 1
        partner_new = (
            jnp.where(use_bit, arrived[0], partner_new[0]),
            jnp.where(use_bit, arrived[1], partner_new[1]),
            jnp.where(use_bit, arrived[2], partner_new[2]),
        )
    new_key = (own_new[0] + partner_new[0]) * 0.5
    new_value = (own_new[1] + partner_new[1]) * 0.5
    new_gain = (own_new[2] + partner_new[2]) * 0.5
    return (keys, values, input_grad, new_key[None], new_value[None], new_gain[None])


def solution(mesh):
    in_specs = (
        P(("rep", "fsdp"), None),
        P("rep", "fsdp"),
        P("rep", "fsdp", None),
        P("rep", "fsdp", None),
        P(("rep", "fsdp"), None),
        P(("rep", "fsdp"), None),
        P(),
        P(),
    )
    out_specs = (
        P(("rep", "fsdp"), None),
        P(("rep", "fsdp"), None),
        P(("rep", "fsdp"), None),
        P("rep", "fsdp", None),
        P("rep", "fsdp", None),
        P("rep", "fsdp"),
    )
    return jax.shard_map(body, mesh=mesh, in_specs=in_specs, out_specs=out_specs, check_vma=False)
```

profile of v0, /device:TPU:1, one launch (start us, length us, event | category | flops | bytes accessed | tf_op | source)
XLA Modules:
  0.0 488.3 jit_solution(6582210835183455542)
XLA Ops:
  7.2 0.7 fusion.21
  7.9 48.4 %all-gather = bf16[32,1,128]{2,1,0:T(2,128)(2,1)S(1)} all-gather(bf16[1,1,128]{2,1,0:T(2,128)(2,1)S(1)} %fusion.21), channel_id=1, replica_groups=mesh['rep'=8,'fsdp'=32] {'fsdp'}, dimensions={0}, use_global_device_ids=true | all-gather | bytes 8448 | tf_op jit(solution)/shard_map/all_gather | solution.py:43
  56.3 3.1 fusion.10
  59.4 6.9 %multiply_convert_fusion.1 = bf16[4096,512]{1,0:T(8,128)(2,1)} fusion(bf16[512,512]{1,0:T(8,128)(2,1)} %param.12, bf16[512,4096]{1,0:T(8,128)(2,1)} %param.8, f32[4096]{0:T(1024)S(1)} %bitcast.53, f32[512]{0:T(512)S(1)} %add_rsqrt_fusion), kind=kOutput, calls=%fused_computation.14 | convolution fusion | flops 2160066560 | bytes 8931328 | tf_op jit(solution)/shard_map/dot_general | solution.py:65
  66.4 6.8 %multiply_convert_fusion = bf16[4096,512]{1,0:T(8,128)(2,1)} fusion(bf16[512,512]{1,0:T(8,128)(2,1)S(1)} %copy-done, bf16[512,4096]{1,0:T(8,128)(2,1)} %param.8, f32[4096]{0:T(1024)S(1)} %bitcast.54, f32[512]{0:T(512)S(1)} %add_rsqrt_fusion), kind=kOutput, calls=%fused_computation.13 | convolution fusion | flops 2160066560 | bytes 8931328 | tf_op jit(solution)/shard_map/dot_general | solution.py:71
  79.3 79.0 %reduce-scatter.3.cloned.1.call-done = bf16[128,512]{1,0:T(8,128)(2,1)} async-done(((bf16[4096,512]{1,0:T(8,128)(2,1)}), bf16[128,512]{1,0:T(8,128)(2,1)}) %reduce-scatter.3.cloned.1.call-update) | async-done | bytes 131088 | tf_op jit(solution)/shard_map/reduce_scatter | solution.py:78
  158.3 0.9 fusion.24
  159.2 1.3 collective-permute-start
  160.5 99.1 %reduce-scatter.5.cloned.1.call-done = bf16[128,512]{1,0:T(8,128)(2,1)} async-done(((bf16[4096,512]{1,0:T(8,128)(2,1)}), bf16[128,512]{1,0:T(8,128)(2,1)}) %reduce-scatter.5.cloned.1.call-update) | async-done | bytes 131088 | tf_op jit(solution)/shard_map/reduce_scatter | solution.py:81
  259.6 0.9 fusion.25
  260.6 1.3 collective-permute-start.3
  261.9 1.0 fusion.13
  262.8 2.5 collective-permute-start.1
  265.3 1.0 fusion.15
  266.3 2.0 collective-permute-start.4
  268.3 1.0 fusion.14
  269.2 0.9 collective-permute-start.2
  270.1 2.9 collective-permute-done.4
  273.0 1.0 fusion.16
  274.3 1.7 multiply_bitcast_fusion.1
  276.0 4.9 %collective-permute-done.5 = bf16[128,512]{1,0:T(8,128)(2,1)S(1)} collective-permute-done((bf16[128,512]{1,0:T(8,128)(2,1)S(1)}, bf16[128,512]{1,0:T(8,128)(2,1)S(1)}, u32[]{:S(2)}, u32[]{:S(2)}) %collective-permute-start.5) | collective-permute-done | bytes 131104 | tf_op jit(solution)/shard_map/ppermute | solution.py:17
  280.9 1.7 multiply_bitcast_fusion
  282.6 40.0 %all-gather.4.cloned.1.call-done = bf16[4096,512]{1,0:T(8,128)(2,1)} async-done(((bf16[128,512]{1,0:T(8,128)(2,1)}), bf16[4096,512]{1,0:T(8,128)(2,1)}) %all-gather.4.cloned.1.call-update) | async-done | bytes 4194320 | tf_op jit(solution)/shard_map/all_gather | solution.py:41
  322.6 7.8 %fusion.33 = f32[512,4096]{1,0:T(8,128)} fusion(bf16[512,512]{1,0:T(8,128)(2,1)S(1)} %copy-done.5, bf16[4096,512]{1,0:T(8,128)(2,1)} %all-gather.4.cloned.1.call-done), kind=kOutput, calls=%fused_computation.53 | convolution fusion | flops 2147483648 | bytes 13107200 | tf_op jit(solution)/shard_map/dot_general | solution.py:49
  330.4 53.1 %all-gather.6.cloned.1.call-done = bf16[4096,512]{1,0:T(8,128)(2,1)} async-done(((bf16[128,512]{1,0:T(8,128)(2,1)}), bf16[4096,512]{1,0:T(8,128)(2,1)}) %all-gather.6.cloned.1.call-update) | async-done | bytes 4194320 | tf_op jit(solution)/shard_map/all_gather | solution.py:42
  383.5 9.5 %fusion.9 = (bf16[4096]{0:T(1024)(128)(2,1)S(1)}, f32[512]{0:T(512)S(1)}, f32[512,4096]{1,0:T(8,128)}) fusion(bf16[512,4096]{1,0:T(8,128)(2,1)} %param.8, f32[512]{0:T(512)S(1)} %add_rsqrt_fusion, f32[4096]{0:T(1024)S(1)} %broadcast_multiply_fusion, f32[512,4096]{1,0:T(8,128)} %fusion.33, bf16[512,512]{1,0:T(8,128)(2,1)S(1)} %copy-done, ...), kind=kOutput, calls=%fused_computation.11 | convolution fusion | flops 2166353408 | bytes 25718784 | tf_op jit(solution)/shard_map/dot_general | solution.py:52
  393.0 70.6 %all-reduce = bf16[4096]{0:T(1024)(128)(2,1)S(1)} all-reduce(bf16[4096]{0:T(1024)(128)(2,1)S(1)} %get-tuple-element.6), channel_id=4, replica_groups=mesh['rep'=8,'fsdp'=32] {'fsdp'}, use_global_device_ids=true, to_apply=%region_5.6.clone | all-reduce | flops 4096 | bytes 16384
  463.7 1.1 collective-permute-start.6
  464.7 7.3 %fusion.8 = bf16[512,4096]{1,0:T(8,128)(2,1)} fusion(bf16[512,4096]{1,0:T(8,128)(2,1)} %param.8, f32[512,4096]{1,0:T(8,128)} %get-tuple-element.12, f32[512]{0:T(512)S(1)} %broadcast_multiply_fusion.1, f32[4096]{0:T(1024)S(1)} %broadcast_multiply_fusion, f32[512]{0:T(512)S(1)} %add_rsqrt_fusion), kind=kLoop, calls=%fused_computation.10 | loop fusion | flops 14680064 | bytes 16797696 | tf_op jit(solution)/shard_map/convert_element_type | solution.py:63
  472.0 2.5 collective-permute-start.7
  474.6 3.2 fusion.11
  478.1 3.2 fusion.12
  (49 shorter events, 4.0 us)
Async XLA Ops:
  7.2 59.2 %copy-start = (bf16[512,512]{1,0:T(8,128)(2,1)S(1)}, bf16[512,512]{1,0:T(8,128)(2,1)}, u32[]{:S(2)}) copy-start(bf16[512,512]{1,0:T(8,128)(2,1)} %param.13) | copy-start | bytes 1572868
  7.2 151.1 %reduce-scatter.3.cloned.1.call-start = ((), (), s32[]{:S(2)}) async-start(), calls=%async_computation.4 | async-start | bytes 4325376 | tf_op jit(solution)/shard_map/reduce_scatter | solution.py:78
  66.3 7.0 %copy-start.2 = (f32[1,128,512]{2,1,0:T(8,128)S(1)}, f32[1,128,512]{2,1,0:T(8,128)}, u32[]{:S(2)}) copy-start(f32[1,128,512]{2,1,0:T(8,128)} %param.10) | copy-start | bytes 786436
  66.3 7.7 %copy-start.3 = (f32[1,128,512]{2,1,0:T(8,128)S(1)}, f32[1,128,512]{2,1,0:T(8,128)}, u32[]{:S(2)}) copy-start(f32[1,128,512]{2,1,0:T(8,128)} %param.11) | copy-start | bytes 786436
  66.3 9.1 %copy-start.8 = (s32[8]{0:T(128)S(1)}, s32[8]{0:T(128)}, u32[]{:S(2)}) copy-start(s32[8]{0:T(128)} %param.15) | copy-start | bytes 100
  66.3 11.7 %copy-start.9 = (u32[256]{0:T(256)S(1)}, u32[256]{0:T(256)}, u32[]{:S(2)}) copy-start(u32[256]{0:T(256)} %constant.63) | copy-start | bytes 3076
  66.4 193.3 %reduce-scatter.5.cloned.1.call-start = ((), (), s32[]{:S(2)}) async-start(), calls=%async_computation.5 | async-start | bytes 4325376 | tf_op jit(solution)/shard_map/reduce_scatter | solution.py:81
  73.2 249.4 %copy-start.5 = (bf16[512,512]{1,0:T(8,128)(2,1)S(1)}, bf16[512,512]{1,0:T(8,128)(2,1)}, u32[]{:S(2)}) copy-start(bf16[512,512]{1,0:T(8,128)(2,1)} %param.12) | copy-start | bytes 1572868
  73.2 249.4 %all-gather.4.cloned.1.call-start = ((), (), s32[]{:S(2)}) async-start(), calls=%async_computation.2 | async-start | bytes 4325376 | tf_op jit(solution)/shard_map/all_gather | solution.py:41
  74.0 309.5 %all-gather.6.cloned.1.call-start = ((), (), s32[]{:S(2)}) async-start(), calls=%async_computation.3 | async-start | bytes 4325376 | tf_op jit(solution)/shard_map/all_gather | solution.py:42
  159.2 102.7 %collective-permute-start = (bf16[128,512]{1,0:T(8,128)(2,1)S(1)}, bf16[128,512]{1,0:T(8,128)(2,1)S(1)}, u32[]{:S(2)}, u32[]{:S(2)}) collective-permute-start(bf16[128,512]{1,0:T(8,128)(2,1)S(1)} %fusion.24), channel_id=1, source_target_pairs={{0,32},{32,0},{64,96},{96,64},{128,160},{160,128},{192,224},{224,1... | collective-permute-start | bytes 393224 | tf_op jit(solution)/shard_map/ppermute | solution.py:17
  260.6 4.8 collective-permute-start.3
  262.8 5.4 %collective-permute-start.1 = (bf16[128,512]{1,0:T(8,128)(2,1)S(1)}, bf16[128,512]{1,0:T(8,128)(2,1)S(1)}, u32[]{:S(2)}, u32[]{:S(2)}) collective-permute-start(bf16[128,512]{1,0:T(8,128)(2,1)S(1)} %fusion.13), channel_id=1, source_target_pairs={{0,64},{32,96},{64,0},{96,32},{128,192},{160,224},{192,128},{224,1... | collective-permute-start | bytes 393224 | tf_op jit(solution)/shard_map/ppermute | solution.py:17
  266.3 6.7 %collective-permute-start.4 = (bf16[128,512]{1,0:T(8,128)(2,1)S(1)}, bf16[128,512]{1,0:T(8,128)(2,1)S(1)}, u32[]{:S(2)}, u32[]{:S(2)}) collective-permute-start(bf16[128,512]{1,0:T(8,128)(2,1)S(1)} %fusion.15), channel_id=1, source_target_pairs={{0,64},{32,96},{64,0},{96,32},{128,192},{160,224},{192,128},{224,1... | collective-permute-start | bytes 393224 | tf_op jit(solution)/shard_map/ppermute | solution.py:17
  269.2 5.0 %collective-permute-start.2 = (bf16[128,512]{1,0:T(8,128)(2,1)S(1)}, bf16[128,512]{1,0:T(8,128)(2,1)S(1)}, u32[]{:S(2)}, u32[]{:S(2)}) collective-permute-start(bf16[128,512]{1,0:T(8,128)(2,1)S(1)} %fusion.14), channel_id=1, source_target_pairs={{0,128},{32,160},{64,192},{96,224},{128,0},{160,32},{192,64},{224,... | collective-permute-start | bytes 393224 | tf_op jit(solution)/shard_map/ppermute | solution.py:17
  274.0 6.9 %collective-permute-start.5 = (bf16[128,512]{1,0:T(8,128)(2,1)S(1)}, bf16[128,512]{1,0:T(8,128)(2,1)S(1)}, u32[]{:S(2)}, u32[]{:S(2)}) collective-permute-start(bf16[128,512]{1,0:T(8,128)(2,1)S(1)} %fusion.16), channel_id=1, source_target_pairs={{0,128},{32,160},{64,192},{96,224},{128,0},{160,32},{192,64},{224,... | collective-permute-start | bytes 393224 | tf_op jit(solution)/shard_map/ppermute | solution.py:17
  330.4 133.2 %copy-start.6 = (f32[1,128]{1,0:T(1,128)S(1)}, f32[1,128]{1,0:T(1,128)}, u32[]{:S(2)}) copy-start(f32[1,128]{1,0:T(1,128)} %param.9) | copy-start | bytes 1540
  463.7 8.4 %collective-permute-start.6 = (bf16[128]{0:T(256)(128)(2,1)S(1)}, bf16[128]{0:T(256)(128)(2,1)S(1)}, u32[]{:S(2)}, u32[]{:S(2)}) collective-permute-start(bf16[128]{0:T(256)(128)(2,1)S(1)} %get-tuple-element.10), channel_id=1, source_target_pairs={{0,32},{32,0},{64,96},{96,64},{128,160},{160,128},{192,224},{224,1... | collective-permute-start | bytes 776 | tf_op jit(solution)/shard_map/ppermute | solution.py:17
  464.7 9.9 %copy-start.1 = (bf16[512,4096]{1,0:T(8,128)(2,1)S(1)}, bf16[512,4096]{1,0:T(8,128)(2,1)}, u32[]{:S(2)}) copy-start(bf16[512,4096]{1,0:T(8,128)(2,1)} %param.8) | copy-start | bytes 12582916
  464.7 9.9 %copy-start.4 = (bf16[4096,512]{1,0:T(8,128)(2,1)S(1)}, bf16[4096,512]{1,0:T(8,128)(2,1)}, u32[]{:S(2)}) copy-start(bf16[4096,512]{1,0:T(8,128)(2,1)} %all-gather.4.cloned.1.call-done) | copy-start | bytes 12582916
  472.0 6.0 %copy-start.7 = (bf16[4096,512]{1,0:T(8,128)(2,1)S(1)}, bf16[4096,512]{1,0:T(8,128)(2,1)}, u32[]{:S(2)}) copy-start(bf16[4096,512]{1,0:T(8,128)(2,1)} %all-gather.6.cloned.1.call-done) | copy-start | bytes 12582916
  472.0 5.8 %collective-permute-start.7 = (bf16[128]{0:T(256)(128)(2,1)S(1)}, bf16[128]{0:T(256)(128)(2,1)S(1)}, u32[]{:S(2)}, u32[]{:S(2)}) collective-permute-start(bf16[128]{0:T(256)(128)(2,1)S(1)} %get-tuple-element.8), channel_id=1, source_target_pairs={{0,64},{32,96},{64,0},{96,32},{128,192},{160,224},{192,128},{224,1... | collective-permute-start | bytes 776 | tf_op jit(solution)/shard_map/ppermute | solution.py:17
  477.8 3.5 collective-permute-start.8
Sparse Core Ops, SparseCore 0:
  66.4 91.7 reduce-scatter.2
  162.7 96.8 reduce-scatter.4
  262.8 59.7 all-gather.3
  325.6 57.8 all-gather.5
where the time goes:
time: 492 us; the launch traced here: 488 us
  waiting for transfers between devices  279 us (57%)
  blocking collectives  119 us (24%)
  matrix products  37.3 us (8%)
  other arithmetic  22.3 us (5%)
  between operations  17.3 us (4%)
  starting transfers between devices  12.2 us (2%)
    reduce_scatter x1, waiting for transfers between devices, body(): lax.psum_scatter(value_term.astype(jnp.bfloat16), 'fsdp', scatter_dimensi...  99.1 us
    reduce_scatter x1, waiting for transfers between devices, body(): lax.psum_scatter(key_term.astype(jnp.bfloat16), 'fsdp', scatter_dimension...  79 us
    unnamed x1, blocking collectives  70.6 us
    all_gather x1, waiting for transfers between devices, body(): value_piece = lax.all_gather(value_b, 'fsdp', axis=0, tiled=True)  53.1 us
    all_gather x1, blocking collectives, body(): gain_piece = lax.all_gather(gain_b, 'fsdp', axis=0, tiled=True)  48.4 us
    all_gather x1, waiting for transfers between devices, body(): key_piece = lax.all_gather(key_b, 'fsdp', axis=0, tiled=True)  40 us
    ppermute x9, starting transfers between devices, swapped(): lax.ppermute(shard, axis, [(i, i ^ 1 << apart) for i in range(lax.axis_si...  12.1 us
  transfers between devices with their start and end apart: 13, of which 6 were waited for; matrix products, arithmetic and copies ran while one was open for 8% of the time, Pallas kernels for 0%

commit v1 on v0

v1 whole, which is shorter than its diff:
```python
import functools

import jax
import jax.numpy as jnp
from jax import lax
from jax.experimental import pallas as pl
from jax.experimental.pallas import tpu as pltpu
from jax.sharding import PartitionSpec as P

MESH = pl.DeviceIdType.MESH
F32 = jnp.float32
BF16 = jnp.bfloat16

lr_weight = 0.25
lr_gain = 0.005

NX = 4
NZ = 4
N_SEND = 96


def kernel(
    act,
    gain_ref,
    kw,
    vw,
    kc,
    vc,
    step_ref,
    plan_ref,
    keys_ref,
    values_ref,
    dn_out,
    coef_ref,
    nk_ref,
    nv_ref,
    ng_ref,
    xv,
    x2h,
    ctv,
    ctT,
    wv,
    gw,
    gs,
    ropp,
    rpl,
    rsm,
    zs,
    rz,
    acc,
    dnb,
    inv_ref,
    own,
    psend,
    precv,
    ssem,
    lsem,
    xsem,
    ctsem,
    agsem,
    sibsem,
    oppsem,
    plsem,
    smsem,
    zsem,
    psem,
    dsem,
):
    me = lax.axis_index("fsdp")
    rep = lax.axis_index("rep")
    zh = me // 8
    xx = (me // 2) % 4
    c = me % 2
    sib = 1 - c

    def at(dz, dx):
        return lax.rem(zh + dz, NZ) * NX + lax.rem(xx + dx, NX)

    def dev(dz, dx, core):
        return (rep, at(dz, dx) * 2 + core)

    sibling = dev(0, 0, sib)
    right = dev(0, 1, c)
    left = dev(0, 3, c)
    partners = [
        (rep + 1 - 2 * (rep % 2), me),
        (rep + 2 - 4 * ((rep // 2) % 2), me),
        (rep + 4 - 8 * ((rep // 4) % 2), me),
    ]
    sends = []

    def send(src, dst, sem, to):
        cp = pltpu.make_async_remote_copy(
            src_ref=src,
            dst_ref=dst,
            send_sem=ssem.at[len(sends)],
            recv_sem=sem,
            device_id=to,
            device_id_type=MESH,
        )
        cp.start()
        sends.append(cp)

    def arrived(dst, sem):
        pltpu.make_async_remote_copy(
            src_ref=dst,
            dst_ref=dst,
            send_sem=ssem.at[0],
            recv_sem=sem,
            device_id=sibling,
            device_id_type=MESH,
        ).wait_recv()

    def local(src, dst, i):
        return pltpu.make_async_copy(src, dst, lsem.at[i])

    l_kw = local(kw.at[0], wv.at[:, pl.ds(0, 512)], 0)
    l_vw = local(vw.at[0], wv.at[:, pl.ds(512, 512)], 1)
    l_x = local(act, xv, 2)
    l_kc = local(kc, ctv.at[:, pl.ds(0, 512)], 3)
    l_vc = local(vc, ctv.at[:, pl.ds(512, 512)], 4)
    for cp in (l_kw, l_vw, l_x, l_kc, l_vc):
        cp.start()

    bar = pltpu.get_barrier_semaphore()
    peers = [sibling, right, left, dev(1, 0, c), dev(2, 0, c), dev(3, 0, c)] + partners
    for to in peers:
        pl.semaphore_signal(bar, inc=1, device_id=to, device_id_type=MESH)
    l_own = []
    for s in (2, 1, 3, 0):
        tx = lax.rem(xx + s, NX)
        for z in range(NZ):
            col = pl.multiple_of(((z * NX + tx) * 2 + c) * 128, 128)
            cp = local(
                act.at[:, pl.ds(col, 128)],
                x2h.at[s, pl.ds(pl.multiple_of(c * 512, 512), 512), pl.ds(z * 128, 128)],
                5 + s * 4 + z,
            )
            cp.start()
            l_own.append(cp)
    pl.semaphore_wait(bar, len(peers))

    l_kw.wait()
    l_vw.wait()
    gain_row = gain_ref[...]
    gain_col = jnp.transpose(jnp.broadcast_to(gain_row, (128, 128)))[:, 0:1]
    mine = gw.at[at(0, 0), pl.ds(pl.multiple_of(c * 128, 128), 128), :]
    mine[...] = (wv[...] * gain_col).astype(BF16)

    def piece(dz, dx):
        return gw.at[at(dz, dx), pl.ds(pl.multiple_of(c * 128, 128), 128), :]

    def sib_piece(dz, dx):
        return gw.at[at(dz, dx), pl.ds(pl.multiple_of(sib * 128, 128), 128), :]

    send(piece(0, 0), piece(0, 0), agsem.at[3], right)
    send(piece(0, 0), piece(0, 0), agsem.at[1], left)
    for dz in (1, 3, 2):
        send(piece(0, 0), piece(0, 0), agsem.at[(4 - dz) * 4], dev(dz, 0, c))

    for s in (2, 1, 3, 0):
        tx = lax.rem(xx + s, NX)
        for z in range(NZ):
            col = pl.multiple_of(((z * NX + tx) * 2 + sib) * 128, 128)
            send(
                act.at[:, pl.ds(col, 128)],
                x2h.at[s, pl.ds(pl.multiple_of(c * 512, 512), 512), pl.ds(z * 128, 128)],
                xsem.at[s],
                sibling,
            )
    send(piece(0, 0), piece(0, 0), sibsem.at[0], sibling)

    l_x.wait()
    l_kc.wait()
    l_vc.wait()

    @pl.loop(0, 4)
    def _(b):
        rows = pl.ds(pl.multiple_of(b * 128, 128), 128)
        xb = xv[rows, :].astype(F32)
        ms = jnp.sum(xb * xb, axis=-1, keepdims=True) * (1.0 / 4096.0)
        inv = lax.rsqrt(ms + 1e-05)
        inv_ref[rows, :] = jnp.broadcast_to(inv, (128, 128))
        lanes = pl.ds(pl.multiple_of(c * 512 + b * 128, 128), 128)
        for r in range(2):
            ct = ctv[rows, r * 512 : (r + 1) * 512].astype(F32) * inv
            ctT[r, :, lanes] = jnp.transpose(ct).astype(BF16)

    own_lanes = pl.ds(pl.multiple_of(c * 512, 512), 512)
    sib_lanes = pl.ds(pl.multiple_of(sib * 512, 512), 512)
    for r in range(2):
        send(ctT.at[r, :, own_lanes], ctT.at[r, :, own_lanes], ctsem.at[r], sibling)
    for cp in l_own:
        cp.wait()

    def grad_block(r, s):
        res = jnp.dot(ctT[r], x2h[s], preferred_element_type=F32)
        for z in range(NZ):
            gs[r, s, z] = res[:, z * 128 : (z + 1) * 128].astype(BF16)

    HA = pl.ds(0, 2)
    HB = pl.ds(2, 2)

    def send_opp(r):
        send(gs.at[r, 2, HA], ropp.at[r, 0], oppsem.at[r * 2], right)
        send(gs.at[r, 2, HB], ropp.at[r, 1], oppsem.at[r * 2 + 1], left)

    def send_plain(r):
        send(gs.at[r, 1, HB], rpl.at[r, 0], plsem.at[r * 2], right)
        send(gs.at[r, 3, HA], rpl.at[r, 1], plsem.at[r * 2 + 1], left)

    def send_summed(r):
        arrived(ropp.at[r, 0], oppsem.at[r * 2])
        for h in range(2):
            gs[r, 1, h] = (gs[r, 1, h].astype(F32) + ropp[r, 0, h].astype(F32)).astype(BF16)
        send(gs.at[r, 1, HA], rsm.at[r, 0], smsem.at[r * 2], right)
        arrived(ropp.at[r, 1], oppsem.at[r * 2 + 1])
        for h in range(2):
            gs[r, 3, 2 + h] = (gs[r, 3, 2 + h].astype(F32) + ropp[r, 1, h].astype(F32)).astype(BF16)
        send(gs.at[r, 3, HB], rsm.at[r, 1], smsem.at[r * 2 + 1], left)

    def x_total(r):
        arrived(rpl.at[r, 0], plsem.at[r * 2])
        arrived(rpl.at[r, 1], plsem.at[r * 2 + 1])
        arrived(rsm.at[r, 0], smsem.at[r * 2])
        arrived(rsm.at[r, 1], smsem.at[r * 2 + 1])
        for h in range(2):
            zs[r, h] = (
                gs[r, 0, h].astype(F32) + rsm[r, 0, h].astype(F32) + rpl[r, 1, h].astype(F32)
            ).astype(BF16)
            zs[r, 2 + h] = (
                gs[r, 0, 2 + h].astype(F32) + rpl[r, 0, h].astype(F32) + rsm[r, 1, h].astype(F32)
            ).astype(BF16)
        for dz in (2, 1, 3):
            send(
                zs.at[r, lax.rem(zh + dz, NZ)],
                rz.at[r, 3 - dz],
                zsem.at[r * 3 + 3 - dz],
                dev(dz, 0, c),
            )

    hop = plan_ref[lax.rem(step_ref[0], 8)]
    gain_part = []

    def update(r):
        total = zs[r, zh].astype(F32)
        for i in range(3):
            arrived(rz.at[r, i], zsem.at[r * 3 + i])
            total = total + rz[r, i].astype(F32)
        grad = jnp.transpose(total) * (1.0 / 64.0)
        w = wv[:, r * 512 : (r + 1) * 512]
        own[r, 0:128, :] = w - lr_weight * gain_col * grad
        gain_part.append(jnp.sum(w.astype(BF16).astype(F32) * grad, axis=-1, keepdims=True))
        if r == 0:
            own[r, 128:144, :] = jnp.zeros((16, 512), F32)
        else:
            gain_sum = jnp.transpose(
                jnp.broadcast_to(gain_part[0] + gain_part[1], (128, 128))
            )[0:1, :]
            new_gain = gain_row - lr_gain * gain_sum
            own[r, 128:144, :] = jnp.broadcast_to(jnp.concatenate([new_gain] * 4, axis=1), (16, 512))
        psend[r, 0] = own[r].astype(BF16)
        swap(r, 0)

    def swap(r, stage):
        send(psend.at[r, stage], precv.at[r, stage], psem.at[r * 3 + stage], partners[stage])

    def swapped(r, stage):
        arrived(precv.at[r, stage], psem.at[r * 3 + stage])
        use = jnp.right_shift(hop, stage) % 2 == 1
        v = jnp.where(use, precv[r, stage].astype(F32), psend[r, stage].astype(F32))
        if stage < 2:
            psend[r, stage + 1] = v.astype(BF16)
            swap(r, stage + 1)
        else:
            o = own[r]
            avg = 0.5 * (o + jnp.where(hop == 0, o, v))
            if r == 0:
                nk_ref[0] = avg[0:128]
            else:
                nv_ref[0] = avg[0:128]
                ng_ref[...] = avg[128:129, 0:128]

    def gathered(dz, dx):
        arrived(piece(dz, dx), agsem.at[dz * 4 + dx])
        send(piece(dz, dx), piece(dz, dx), sibsem.at[dz * 4 + dx], sibling)

    def pairs(first, items):
        for n, (dz, dx) in enumerate(items):
            arrived(sib_piece(dz, dx), sibsem.at[dz * 4 + dx])
        for n, (dz, dx) in enumerate(items):
            j = at(dz, dx)
            cols = pl.ds(pl.multiple_of(j * 256, 256), 256)

            @pl.loop(0, 2)
            def _(b):
                rows = pl.ds(pl.multiple_of(b * 256, 256), 256)
                part = jnp.dot(xv[rows, cols], gw[j], preferred_element_type=F32)
                if first and n == 0:
                    acc[rows, :] = part
                else:
                    acc[rows, :] += part
                d = lax.dot_general(
                    ctv[rows, :], gw[j], (((1,), (1,)), ((), ())), preferred_element_type=F32
                )
                dnb[rows, cols] = (d * (inv_ref[rows, 0:1] * (1.0 / 64.0))).astype(BF16)

            pltpu.make_async_copy(dnb.at[:, cols], dn_out.at[:, cols], dsem).start()

    arrived(ctT.at[0, :, sib_lanes], ctsem.at[0])
    for s in (2, 1, 3, 0):
        arrived(x2h.at[s, sib_lanes, :], xsem.at[s])
    grad_block(0, 2)
    send_opp(0)
    grad_block(0, 1)
    grad_block(0, 3)
    send_plain(0)
    arrived(ctT.at[1, :, sib_lanes], ctsem.at[1])
    grad_block(1, 2)
    grad_block(1, 1)
    grad_block(1, 3)
    grad_block(0, 0)
    grad_block(1, 0)
    send_summed(0)
    send_opp(1)
    send_plain(1)
    pairs(True, [(0, 0)])
    gathered(0, 1)
    gathered(0, 3)
    pairs(False, [(0, 1), (0, 3)])
    gathered(1, 0)
    gathered(3, 0)
    x_total(0)
    gathered(2, 0)
    send_summed(1)
    send(piece(0, 3), piece(0, 3), agsem.at[2], right)
    for dr, dl in ((1, 3), (3, 2), (2, 1)):
        send(piece(dr, 0), piece(dr, 0), agsem.at[dr * 4 + 3], right)
        send(piece(dl, 0), piece(dl, 0), agsem.at[dl * 4 + 1], left)
    pairs(False, [(1, 0), (3, 0), (2, 0)])
    update(0)
    swapped(0, 0)
    x_total(1)
    swapped(0, 1)
    swapped(0, 2)
    update(1)
    gathered(1, 3)
    send(piece(1, 3), piece(1, 3), agsem.at[4 + 2], right)
    gathered(3, 1)
    send(piece(3, 1), piece(3, 1), agsem.at[12 + 2], left)
    gathered(2, 1)
    send(piece(2, 1), piece(2, 1), agsem.at[8 + 2], left)
    gathered(0, 2)
    swapped(1, 0)
    pairs(False, [(1, 3), (3, 1), (2, 1), (0, 2)])
    swapped(1, 1)
    gathered(3, 3)
    gathered(2, 3)
    gathered(1, 1)
    pairs(False, [(3, 3), (2, 3), (1, 1)])
    swapped(1, 2)
    gathered(3, 2)
    gathered(1, 2)
    pairs(False, [(3, 2), (1, 2)])
    gathered(2, 2)
    pairs(False, [(2, 2)])

    @pl.loop(0, 4)
    def _(b):
        rows = pl.ds(pl.multiple_of(b * 128, 128), 128)
        inv = inv_ref[rows, 0:1]
        kv = acc[rows, :] * (inv * (1.0 / 64.0))
        inner = jnp.sum(kv * ctv[rows, :].astype(F32), axis=-1, keepdims=True) * (1.0 / 4096.0)
        keys_ref[rows, :] = kv[:, 0:512].astype(BF16)
        values_ref[rows, :] = kv[:, 512:1024].astype(BF16)
        coef_ref[rows, :] = jnp.broadcast_to(inv * inv * inner, (128, 128))

    for cp in sends:
        cp.wait_send()
    pltpu.make_async_copy(dnb, dn_out, dsem).wait()


def body(
    activations,
    norm_gain,
    key_weight,
    value_weight,
    key_cotangent,
    value_cotangent,
    step_index,
    plan,
):
    any_spec = pl.BlockSpec(memory_space=pl.ANY)
    vmem = pl.BlockSpec(memory_space=pltpu.VMEM)
    smem = pl.BlockSpec(memory_space=pltpu.SMEM)
    shape = jax.ShapeDtypeStruct
    V = pltpu.VMEM
    DMA = pltpu.SemaphoreType.DMA
    keys, values, dn, coef, nk, nv, ng = pl.pallas_call(
        kernel,
        name="group_step",
        out_shape=(
            shape((512, 512), BF16),
            shape((512, 512), BF16),
            shape((512, 4096), BF16),
            shape((512, 128), F32),
            shape((1, 128, 512), F32),
            shape((1, 128, 512), F32),
            shape((1, 128), F32),
        ),
        in_specs=[any_spec, vmem, any_spec, any_spec, any_spec, any_spec, smem, smem],
        out_specs=(vmem, vmem, any_spec, vmem, vmem, vmem, vmem),
        scratch_shapes=[
            V((512, 4096), BF16),
            V((4, 1024, 512), BF16),
            V((512, 1024), BF16),
            V((2, 512, 1024), BF16),
            V((128, 1024), F32),
            V((16, 256, 1024), BF16),
            V((2, 4, 4, 512, 128), BF16),
            V((2, 2, 2, 512, 128), BF16),
            V((2, 2, 2, 512, 128), BF16),
            V((2, 2, 2, 512, 128), BF16),
            V((2, 4, 512, 128), BF16),
            V((2, 3, 512, 128), BF16),
            V((512, 1024), F32),
            V((512, 4096), BF16),
            V((512, 128), F32),
            V((2, 144, 512), F32),
            V((2, 3, 144, 512), BF16),
            V((2, 3, 144, 512), BF16),
            DMA((N_SEND,)),
            DMA((24,)),
            DMA((4,)),
            DMA((2,)),
            DMA((16,)),
            DMA((16,)),
            DMA((4,)),
            DMA((4,)),
            DMA((4,)),
            DMA((6,)),
            DMA((6,)),
            DMA,
        ],
        compiler_params=pltpu.CompilerParams(
            collective_id=0, has_side_effects=True, vmem_limit_bytes=58 << 20
        ),
        cost_estimate=pl.CostEstimate(
            flops=13_000_000_000, bytes_accessed=24 << 20, transcendentals=512
        ),
    )(
        activations,
        norm_gain,
        key_weight,
        value_weight,
        key_cotangent,
        value_cotangent,
        step_index,
        plan,
    )
    input_grad = (dn.astype(F32) - activations.astype(F32) * coef[:, 0:1]).astype(BF16)
    return keys, values, input_grad, nk, nv, ng


def solution(mesh):
    in_specs = (
        P(("rep", "fsdp"), None),
        P("rep", "fsdp"),
        P("rep", "fsdp", None),
        P("rep", "fsdp", None),
        P(("rep", "fsdp"), None),
        P(("rep", "fsdp"), None),
        P(),
        P(),
    )
    out_specs = (
        P(("rep", "fsdp"), None),
        P(("rep", "fsdp"), None),
        P(("rep", "fsdp"), None),
        P("rep", "fsdp", None),
        P("rep", "fsdp", None),
        P("rep", "fsdp"),
    )
    return jax.shard_map(body, mesh=mesh, in_specs=in_specs, out_specs=out_specs, check_vma=False)
```

time: 492 us -> 110 us (0.22)
  waiting for transfers between devices: 279 us -> 0 us
  blocking collectives: 119 us -> 0 us
  Pallas kernels: 0 us -> 97.1 us
  matrix products: 37.3 us -> 0 us
  between operations: 17.3 us -> 1.35 us
  other arithmetic: 22.3 us -> 6.48 us
  starting transfers between devices: 12.2 us -> 0 us
    reduce_scatter x2 -> x0, waiting for transfers between devices: 178 us -> none  [the longest x1 99.1 us: body(): lax.psum_scatter(value_term.astype(jnp.bfloat16), 'fsdp', scatter_dimensi...]
    pallas_call x0 -> x1, Pallas kernels: none -> 97.1 us  [body(): pl.pallas_call(kernel, name='group_step', out_shape=(shape((512, 512), BF...]
    all_gather x2 -> x0, waiting for transfers between devices: 93.1 us -> none  [the longest x1 53.1 us: body(): value_piece = lax.all_gather(value_b, 'fsdp', axis=0, tiled=True)]
    unnamed x1 -> x0, blocking collectives: 70.6 us -> none
    all_gather x1 -> x0, blocking collectives: 48.4 us -> none  [body(): gain_piece = lax.all_gather(gain_b, 'fsdp', axis=0, tiled=True)]
    dot_general x6 -> x0, matrix products: 37.3 us -> none  [the longest x1 9.47 us: body(): lax.dot_general(value_cotangent, value_piece, (((1,), (1,)), ((), ())), p...]
    ppermute x9 -> x0, starting transfers between devices: 12.1 us -> none  [swapped(): lax.ppermute(shard, axis, [(i, i ^ 1 << apart) for i in range(lax.axis_si...]
    convert_element_type x13 -> x1, other arithmetic: 14.5 us -> 6.48 us  [body(): (dn.astype(F32) - activations.astype(F32) * coef[:, 0:1]).astype(BF16)]
  transfers between devices with their start and end apart: 13 -> 0, of which waited for: 6 -> 0; matrix products, arithmetic and copies ran while one was open for 8% -> 0% of each run, Pallas kernels for 0% -> 0%
where the time goes in v1:
time: 110 us
  Pallas kernels  97.1 us (88%)
  other arithmetic  6.48 us (6%)
  local copies, waits for them, and re-layouts  4.62 us (4%)
  between operations  1.35 us (1%)
    pallas_call x1, Pallas kernels, body(): pl.pallas_call(kernel, name='group_step', out_shape=(shape((512, 512), BF...  97.1 us
    convert_element_type x1, other arithmetic, body(): (dn.astype(F32) - activations.astype(F32) * coef[:, 0:1]).astype(BF16)  6.48 us
    unnamed x17, local copies, waits for them, and re-layouts  3.53 us

profile of v1, /device:TPU:1, one launch (start us, length us, event | category | flops | bytes accessed | tf_op | source)
XLA Modules:
  0.0 109.6 jit_solution(3547747936548785055)
XLA Ops:
  1.3 0.0 copy-start
  1.3 97.1 %group_step.1 = (bf16[512,512]{1,0:T(8,128)(2,1)}, bf16[512,512]{1,0:T(8,128)(2,1)}, bf16[512,4096]{1,0:T(8,128)(2,1)}, f32[512,128]{1,0:T(8,128)}, f32[1,128,51...) custom-call(bf16[512,4096]{1,0:T(8,128)(2,1)} %act.1, f32[1,128]{1,0:T(1,128)} %gain_ref.1, ...), custom_call_target="tpu_custom_call" | custom-call | flops 12999999488 | bytes 25165824 | tf_op jit(solution)/shard_map/group_step/pallas_call | solution.py:399
  98.4 1.1 slice_reduce_fusion
  99.5 0.0 copy-done
  99.5 0.0 copy-start.2
  99.5 0.0 copy-start.1
  99.5 0.0 copy-start.4
  99.5 0.0 copy-start.3
  99.6 0.0 copy-start.5
  99.6 6.5 %subtract_convert_fusion = bf16[512,4096]{1,0:T(8,128)(2,1)} fusion(bf16[512,4096]{1,0:T(8,128)(2,1)S(1)} %copy-done, bf16[512,4096]{1,0:T(8,128)(2,1)} %get-tuple-element.15, f32[512]{0:T(512)S(1)} %slice_reduce_fusion), kind=kLoop, calls=%fused_computation | loop fusion | flops 10485760 | bytes 12584960 | tf_op jit(solution)/shard_map/convert_element_type | solution.py:461
  106.0 0.0 copy-done.2
  106.0 0.8 copy.20
  106.8 0.0 copy-done.1
  106.8 0.8 copy.21
  107.6 0.0 copy-done.4
  107.6 0.7 copy.22
  108.3 0.0 copy-done.3
  108.3 0.7 copy.23
  109.0 0.0 copy-done.5
  109.1 0.5 copy.24
Async XLA Ops:
  1.3 98.2 %copy-start = (bf16[512,4096]{1,0:T(8,128)(2,1)S(1)}, bf16[512,4096]{1,0:T(8,128)(2,1)}, u32[]{:S(2)}) copy-start(bf16[512,4096]{1,0:T(8,128)(2,1)} %act.1) | copy-start | bytes 12582916
  99.5 6.5 %copy-start.2 = (bf16[512,512]{1,0:T(8,128)(2,1)S(1)}, bf16[512,512]{1,0:T(8,128)(2,1)}, u32[]{:S(2)}) copy-start(bf16[512,512]{1,0:T(8,128)(2,1)} %get-tuple-element.26) | copy-start | bytes 1572868
  99.5 7.3 %copy-start.1 = (bf16[512,512]{1,0:T(8,128)(2,1)S(1)}, bf16[512,512]{1,0:T(8,128)(2,1)}, u32[]{:S(2)}) copy-start(bf16[512,512]{1,0:T(8,128)(2,1)} %get-tuple-element.27) | copy-start | bytes 1572868
  99.5 8.1 %copy-start.4 = (f32[1,128,512]{2,1,0:T(8,128)S(1)}, f32[1,128,512]{2,1,0:T(8,128)}, u32[]{:S(2)}) copy-start(f32[1,128,512]{2,1,0:T(8,128)} %get-tuple-element.29) | copy-start | bytes 786436
  99.5 8.8 %copy-start.3 = (f32[1,128,512]{2,1,0:T(8,128)S(1)}, f32[1,128,512]{2,1,0:T(8,128)}, u32[]{:S(2)}) copy-start(f32[1,128,512]{2,1,0:T(8,128)} %get-tuple-element.30) | copy-start | bytes 786436
  99.6 9.5 %copy-start.5 = (f32[1,128]{1,0:T(1,128)S(1)}, f32[1,128]{1,0:T(1,128)}, u32[]{:S(2)}) copy-start(f32[1,128]{1,0:T(1,128)} %get-tuple-element.31) | copy-start | bytes 1540

commit v2 on v1

--- a/solution.py
+++ b/solution.py
@@ -1,5 +1,3 @@
-import functools
-
 import jax
 import jax.numpy as jnp
 from jax import lax
@@ -14,26 +12,36 @@
 lr_weight = 0.25
 lr_gain = 0.005
 
+FINISH = 8
+FROWS = 512 // FINISH
 NX = 4
 NZ = 4
-N_SEND = 96
+N_SEND = 128
+ROUNDS = 4
+KR = 1024 // ROUNDS
 
 
 def kernel(
     act,
-    gain_ref,
+    gain_in,
     kw,
     vw,
     kc,
     vc,
-    step_ref,
-    plan_ref,
+    step_in,
+    plan_in,
+    keys_out,
+    values_out,
+    dn_out,
+    coef_out,
+    nk_out,
+    nv_out,
+    ng_out,
     keys_ref,
     values_ref,
-    dn_out,
+    dn_ref,
     coef_ref,
-    nk_ref,
-    nv_ref,
+    nw_ref,
     ng_ref,
     xv,
     x2h,
@@ -48,7 +56,9 @@
     zs,
     rz,
     acc,
-    dnb,
+    gain_ref,
+    step_ref,
+    plan_ref,
     inv_ref,
     own,
     psend,
@@ -58,6 +68,7 @@
     xsem,
     ctsem,
     agsem,
+    agh,
     sibsem,
     oppsem,
     plsem,
@@ -65,6 +76,7 @@
     zsem,
     psem,
     dsem,
+    osem,
 ):
     me = lax.axis_index("fsdp")
     rep = lax.axis_index("rep")
@@ -82,10 +94,12 @@
     sibling = dev(0, 0, sib)
     right = dev(0, 1, c)
     left = dev(0, 3, c)
+    bit0, bit1, bit2 = rep % 2, (rep // 2) % 2, (rep // 4) % 2
     partners = [
-        (rep + 1 - 2 * (rep % 2), me),
-        (rep + 2 - 4 * ((rep // 2) % 2), me),
-        (rep + 4 - 8 * ((rep // 4) % 2), me),
+        (rep + 1 - 2 * bit0, me),
+        (rep + 2 - 4 * bit1, me),
+        (rep + 3 - 2 * bit0 - 4 * bit1, me),
+        (rep + 4 - 8 * bit2, me),
     ]
     sends = []
 
@@ -119,8 +133,18 @@
     l_x = local(act, xv, 2)
     l_kc = local(kc, ctv.at[:, pl.ds(0, 512)], 3)
     l_vc = local(vc, ctv.at[:, pl.ds(512, 512)], 4)
-    for cp in (l_kw, l_vw, l_x, l_kc, l_vc):
+    l_gain = local(gain_in, gain_ref, 21)
+    l_step = local(step_in, step_ref, 22)
+    l_plan = local(plan_in, plan_ref, 23)
+    for cp in (l_gain, l_kw, l_vw, l_x, l_kc, l_vc, l_step, l_plan):
         cp.start()
+
+    outs = []
+
+    def out(src, dst):
+        cp = pltpu.make_async_copy(src, dst, osem.at[len(outs)])
+        cp.start()
+        outs.append(cp)
 
     bar = pltpu.get_barrier_semaphore()
     peers = [sibling, right, left, dev(1, 0, c), dev(2, 0, c), dev(3, 0, c)] + partners
@@ -140,6 +164,7 @@
             l_own.append(cp)
     pl.semaphore_wait(bar, len(peers))
 
+    l_gain.wait()
     l_kw.wait()
     l_vw.wait()
     gain_row = gain_ref[...]
@@ -182,13 +207,13 @@
         inv = lax.rsqrt(ms + 1e-05)
         inv_ref[rows, :] = jnp.broadcast_to(inv, (128, 128))
         lanes = pl.ds(pl.multiple_of(c * 512 + b * 128, 128), 128)
-        for r in range(2):
-            ct = ctv[rows, r * 512 : (r + 1) * 512].astype(F32) * inv
+        for r in range(ROUNDS):
+            ct = ctv[rows, r * KR : (r + 1) * KR].astype(F32) * inv
             ctT[r, :, lanes] = jnp.transpose(ct).astype(BF16)
 
     own_lanes = pl.ds(pl.multiple_of(c * 512, 512), 512)
     sib_lanes = pl.ds(pl.multiple_of(sib * 512, 512), 512)
-    for r in range(2):
+    for r in range(ROUNDS):
         send(ctT.at[r, :, own_lanes], ctT.at[r, :, own_lanes], ctsem.at[r], sibling)
     for cp in l_own:
         cp.wait()
@@ -202,6 +227,7 @@
     HB = pl.ds(2, 2)
 
     def send_opp(r):
+        grad_block(r, 2)
         send(gs.at[r, 2, HA], ropp.at[r, 0], oppsem.at[r * 2], right)
         send(gs.at[r, 2, HB], ropp.at[r, 1], oppsem.at[r * 2 + 1], left)
 
@@ -218,6 +244,16 @@
         for h in range(2):
             gs[r, 3, 2 + h] = (gs[r, 3, 2 + h].astype(F32) + ropp[r, 1, h].astype(F32)).astype(BF16)
         send(gs.at[r, 3, HB], rsm.at[r, 1], smsem.at[r * 2 + 1], left)
+
+    def step(r):
+        send_summed(r)
+        if r + 1 < ROUNDS:
+            send_plain(r + 1)
+        if r + 2 < ROUNDS:
+            send_opp(r + 2)
+            grad_block(r + 2, 1)
+            grad_block(r + 2, 3)
+            grad_block(r + 2, 0)
 
     def x_total(r):
         arrived(rpl.at[r, 0], plsem.at[r * 2])
@@ -231,7 +267,7 @@
             zs[r, 2 + h] = (
                 gs[r, 0, 2 + h].astype(F32) + rpl[r, 0, h].astype(F32) + rsm[r, 1, h].astype(F32)
             ).astype(BF16)
-        for dz in (2, 1, 3):
+        for dz in (1, 3, 2):
             send(
                 zs.at[r, lax.rem(zh + dz, NZ)],
                 rz.at[r, 3 - dz],
@@ -239,6 +275,8 @@
                 dev(dz, 0, c),
             )
 
+    l_step.wait()
+    l_plan.wait()
     hop = plan_ref[lax.rem(step_ref[0], 8)]
     gain_part = []
 
@@ -248,41 +286,61 @@
             arrived(rz.at[r, i], zsem.at[r * 3 + i])
             total = total + rz[r, i].astype(F32)
         grad = jnp.transpose(total) * (1.0 / 64.0)
-        w = wv[:, r * 512 : (r + 1) * 512]
+        w = wv[:, r * KR : (r + 1) * KR]
         own[r, 0:128, :] = w - lr_weight * gain_col * grad
         gain_part.append(jnp.sum(w.astype(BF16).astype(F32) * grad, axis=-1, keepdims=True))
-        if r == 0:
-            own[r, 128:144, :] = jnp.zeros((16, 512), F32)
+        if r < ROUNDS - 1:
+            own[r, 128:144, :] = jnp.zeros((16, KR), F32)
         else:
-            gain_sum = jnp.transpose(
-                jnp.broadcast_to(gain_part[0] + gain_part[1], (128, 128))
-            )[0:1, :]
+            gain_sum = jnp.transpose(jnp.broadcast_to(sum(gain_part), (128, 128)))[0:1, :]
             new_gain = gain_row - lr_gain * gain_sum
-            own[r, 128:144, :] = jnp.broadcast_to(jnp.concatenate([new_gain] * 4, axis=1), (16, 512))
+            own[r, 128:144, :] = jnp.broadcast_to(
+                jnp.concatenate([new_gain] * (KR // 128), axis=1), (16, KR)
+            )
         psend[r, 0] = own[r].astype(BF16)
-        swap(r, 0)
-
-    def swap(r, stage):
-        send(psend.at[r, stage], precv.at[r, stage], psem.at[r * 3 + stage], partners[stage])
-
-    def swapped(r, stage):
-        arrived(precv.at[r, stage], psem.at[r * 3 + stage])
-        use = jnp.right_shift(hop, stage) % 2 == 1
-        v = jnp.where(use, precv[r, stage].astype(F32), psend[r, stage].astype(F32))
-        if stage < 2:
-            psend[r, stage + 1] = v.astype(BF16)
-            swap(r, stage + 1)
+        for i in range(3):
+            send(psend.at[r, 0], precv.at[r, i], psem.at[r * 4 + i], partners[i])
+
+    def swap_y(r):
+        v = psend[r, 0].astype(F32)
+        low = hop % 4
+        for i in range(3):
+            arrived(precv.at[r, i], psem.at[r * 4 + i])
+            v = jnp.where(low == i + 1, precv[r, i].astype(F32), v)
+        psend[r, 1] = v.astype(BF16)
+        send(psend.at[r, 1], precv.at[r, 3], psem.at[r * 4 + 3], partners[3])
+
+    def swap_z(r):
+        arrived(precv.at[r, 3], psem.at[r * 4 + 3])
+        v = jnp.where(hop >= 4, precv[r, 3].astype(F32), psend[r, 1].astype(F32))
+        o = own[r]
+        avg = 0.5 * (o + jnp.where(hop == 0, o, v))
+        nw_ref[:, r * KR : (r + 1) * KR] = avg[0:128]
+        half = ROUNDS // 2
+        if r == half - 1:
+            out(nw_ref.at[:, pl.ds(0, 512)], nk_out.at[0])
+        if r == ROUNDS - 1:
+            out(nw_ref.at[:, pl.ds(512, 512)], nv_out.at[0])
+            ng_ref[...] = avg[128:129, 0:128]
+            out(ng_ref, ng_out)
+
+    def rows_of(dz, dx, lo, n):
+        return gw.at[at(dz, dx), pl.ds(pl.multiple_of(c * 128 + lo, 16), n), :]
+
+    def forward_right(dz, lo, n):
+        send(rows_of(dz, 3, lo, n), rows_of(dz, 3, lo, n), agsem.at[dz * 4 + 2], right)
+
+    def forward_left(dz, lo, n):
+        sem = agsem if n == 128 else agh
+        k = dz * 4 + 2 if n == 128 else dz
+        send(rows_of(dz, 1, lo, n), rows_of(dz, 1, lo, n), sem.at[k], left)
+
+    def gathered(dz, dx):
+        if dx == 2 and dz % 2 == 0:
+            arrived(rows_of(dz, dx, 0, 64), agsem.at[dz * 4 + dx])
+            arrived(rows_of(dz, dx, 64, 64), agh.at[dz])
         else:
-            o = own[r]
-            avg = 0.5 * (o + jnp.where(hop == 0, o, v))
-            if r == 0:
-                nk_ref[0] = avg[0:128]
-            else:
-                nv_ref[0] = avg[0:128]
-                ng_ref[...] = avg[128:129, 0:128]
-
-    def gathered(dz, dx):
-        arrived(piece(dz, dx), agsem.at[dz * 4 + dx])
+            arrived(piece(dz, dx), agsem.at[dz * 4 + dx])
         send(piece(dz, dx), piece(dz, dx), sibsem.at[dz * 4 + dx], sibling)
 
     def pairs(first, items):
@@ -303,81 +361,95 @@
                 d = lax.dot_general(
                     ctv[rows, :], gw[j], (((1,), (1,)), ((), ())), preferred_element_type=F32
                 )
-                dnb[rows, cols] = (d * (inv_ref[rows, 0:1] * (1.0 / 64.0))).astype(BF16)
-
-            pltpu.make_async_copy(dnb.at[:, cols], dn_out.at[:, cols], dsem).start()
-
-    arrived(ctT.at[0, :, sib_lanes], ctsem.at[0])
+                dn_ref[rows, cols] = (d * (inv_ref[rows, 0:1] * (1.0 / 64.0))).astype(BF16)
+
+            pltpu.make_async_copy(dn_ref.at[:, cols], dn_out.at[:, cols], dsem).start()
+
+    for r in range(ROUNDS):
+        arrived(ctT.at[r, :, sib_lanes], ctsem.at[r])
     for s in (2, 1, 3, 0):
         arrived(x2h.at[s, sib_lanes, :], xsem.at[s])
-    grad_block(0, 2)
     send_opp(0)
     grad_block(0, 1)
     grad_block(0, 3)
     send_plain(0)
-    arrived(ctT.at[1, :, sib_lanes], ctsem.at[1])
-    grad_block(1, 2)
+    send_opp(1)
     grad_block(1, 1)
     grad_block(1, 3)
+    step(0)
     grad_block(0, 0)
     grad_block(1, 0)
-    send_summed(0)
-    send_opp(1)
-    send_plain(1)
-    pairs(True, [(0, 0)])
     gathered(0, 1)
     gathered(0, 3)
+    pairs(True, [(0, 0)])
+    step(1)
+    x_total(0)
     pairs(False, [(0, 1), (0, 3)])
     gathered(1, 0)
     gathered(3, 0)
-    x_total(0)
+    pairs(False, [(1, 0), (3, 0)])
+    step(2)
     gathered(2, 0)
-    send_summed(1)
-    send(piece(0, 3), piece(0, 3), agsem.at[2], right)
-    for dr, dl in ((1, 3), (3, 2), (2, 1)):
+    update(0)
+    x_total(1)
+    pairs(False, [(2, 0)])
+    swap_y(0)
+    step(3)
+    forward_left(0, 64, 64)
+    forward_right(0, 0, 64)
+    for dr, dl in ((1, 3), (2, 2), (3, 1)):
         send(piece(dr, 0), piece(dr, 0), agsem.at[dr * 4 + 3], right)
         send(piece(dl, 0), piece(dl, 0), agsem.at[dl * 4 + 1], left)
-    pairs(False, [(1, 0), (3, 0), (2, 0)])
-    update(0)
-    swapped(0, 0)
-    x_total(1)
-    swapped(0, 1)
-    swapped(0, 2)
+    swap_z(0)
     update(1)
+    x_total(2)
+    swap_y(1)
+    x_total(3)
+    swap_z(1)
+    update(2)
+    gathered(0, 2)
+    pairs(False, [(0, 2)])
+    swap_y(2)
+    update(3)
     gathered(1, 3)
-    send(piece(1, 3), piece(1, 3), agsem.at[4 + 2], right)
+    forward_right(1, 0, 128)
     gathered(3, 1)
-    send(piece(3, 1), piece(3, 1), agsem.at[12 + 2], left)
+    forward_left(3, 0, 128)
+    swap_z(2)
+    pairs(False, [(1, 3), (3, 1)])
+    swap_y(3)
+    gathered(2, 3)
+    forward_right(2, 0, 64)
     gathered(2, 1)
-    send(piece(2, 1), piece(2, 1), agsem.at[8 + 2], left)
-    gathered(0, 2)
-    swapped(1, 0)
-    pairs(False, [(1, 3), (3, 1), (2, 1), (0, 2)])
-    swapped(1, 1)
+    forward_left(2, 64, 64)
+    swap_z(3)
+    pairs(False, [(2, 3), (2, 1)])
     gathered(3, 3)
-    gathered(2, 3)
     gathered(1, 1)
-    pairs(False, [(3, 3), (2, 3), (1, 1)])
-    swapped(1, 2)
+    pairs(False, [(3, 3), (1, 1)])
+    gathered(1, 2)
     gathered(3, 2)
-    gathered(1, 2)
-    pairs(False, [(3, 2), (1, 2)])
+    pairs(False, [(1, 2), (3, 2)])
     gathered(2, 2)
     pairs(False, [(2, 2)])
 
-    @pl.loop(0, 4)
-    def _(b):
-        rows = pl.ds(pl.multiple_of(b * 128, 128), 128)
+    for b in range(4):
+        rows = pl.ds(b * 128, 128)
         inv = inv_ref[rows, 0:1]
         kv = acc[rows, :] * (inv * (1.0 / 64.0))
         inner = jnp.sum(kv * ctv[rows, :].astype(F32), axis=-1, keepdims=True) * (1.0 / 4096.0)
         keys_ref[rows, :] = kv[:, 0:512].astype(BF16)
         values_ref[rows, :] = kv[:, 512:1024].astype(BF16)
         coef_ref[rows, :] = jnp.broadcast_to(inv * inv * inner, (128, 128))
+        out(keys_ref.at[rows, :], keys_out.at[rows, :])
+        out(values_ref.at[rows, :], values_out.at[rows, :])
+        out(coef_ref.at[rows, :], coef_out.at[rows, :])
 
     for cp in sends:
         cp.wait_send()
-    pltpu.make_async_copy(dnb, dn_out, dsem).wait()
+    for cp in outs:
+        cp.wait()
+    pltpu.make_async_copy(dn_ref, dn_out, dsem).wait()
 
 
 def body(
@@ -390,9 +462,7 @@
     step_index,
     plan,
 ):
-    any_spec = pl.BlockSpec(memory_space=pl.ANY)
-    vmem = pl.BlockSpec(memory_space=pltpu.VMEM)
-    smem = pl.BlockSpec(memory_space=pltpu.SMEM)
+    hbm = pl.BlockSpec(memory_space=pltpu.HBM)
     shape = jax.ShapeDtypeStruct
     V = pltpu.VMEM
     DMA = pltpu.SemaphoreType.DMA
@@ -408,39 +478,49 @@
             shape((1, 128, 512), F32),
             shape((1, 128), F32),
         ),
-        in_specs=[any_spec, vmem, any_spec, any_spec, any_spec, any_spec, smem, smem],
-        out_specs=(vmem, vmem, any_spec, vmem, vmem, vmem, vmem),
+        in_specs=[hbm] * 8,
+        out_specs=(hbm,) * 7,
         scratch_shapes=[
+            V((512, 512), BF16),
+            V((512, 512), BF16),
+            V((512, 4096), BF16),
+            V((512, 128), F32),
+            V((128, 1024), F32),
+            V((1, 128), F32),
             V((512, 4096), BF16),
             V((4, 1024, 512), BF16),
             V((512, 1024), BF16),
-            V((2, 512, 1024), BF16),
+            V((ROUNDS, KR, 1024), BF16),
             V((128, 1024), F32),
             V((16, 256, 1024), BF16),
-            V((2, 4, 4, 512, 128), BF16),
-            V((2, 2, 2, 512, 128), BF16),
-            V((2, 2, 2, 512, 128), BF16),
-            V((2, 2, 2, 512, 128), BF16),
-            V((2, 4, 512, 128), BF16),
-            V((2, 3, 512, 128), BF16),
+            V((ROUNDS, 4, 4, KR, 128), BF16),
+            V((ROUNDS, 2, 2, KR, 128), BF16),
+            V((ROUNDS, 2, 2, KR, 128), BF16),
+            V((ROUNDS, 2, 2, KR, 128), BF16),
+            V((ROUNDS, 4, KR, 128), BF16),
+            V((ROUNDS, 3, KR, 128), BF16),
             V((512, 1024), F32),
-            V((512, 4096), BF16),
+            V((1, 128), F32),
+            pltpu.SMEM((1,), jnp.int32),
+            pltpu.SMEM((8,), jnp.int32),
             V((512, 128), F32),
-            V((2, 144, 512), F32),
-            V((2, 3, 144, 512), BF16),
-            V((2, 3, 144, 512), BF16),
+            V((ROUNDS, 144, KR), F32),
+            V((ROUNDS, 2, 144, KR), BF16),
+            V((ROUNDS, 4, 144, KR), BF16),
             DMA((N_SEND,)),
             DMA((24,)),
             DMA((4,)),
-            DMA((2,)),
-            DMA((16,)),
+            DMA((ROUNDS,)),
             DMA((16,)),
             DMA((4,)),
-            DMA((4,)),
-            DMA((4,)),
-            DMA((6,)),
-            DMA((6,)),
+            DMA((16,)),
+            DMA((2 * ROUNDS,)),
+            DMA((2 * ROUNDS,)),
+            DMA((2 * ROUNDS,)),
+            DMA((3 * ROUNDS,)),
+            DMA((4 * ROUNDS,)),
             DMA,
+            DMA((20,)),
         ],
         compiler_params=pltpu.CompilerParams(
             collective_id=0, has_side_effects=True, vmem_limit_bytes=58 << 20
@@ -458,8 +538,88 @@
         step_index,
         plan,
     )
-    input_grad = (dn.astype(F32) - activations.astype(F32) * coef[:, 0:1]).astype(BF16)
-    return keys, values, input_grad, nk, nv, ng
+    return finish(activations, dn, coef, keys, values, nk, nv, ng)
+
+
+def finish_kernel(
+    act, dn, coef, keys, values, nk, nv, ng, grad_o, k_o, v_o, nk_o, nv_o, ng_o,
+    cv, dv, av, out, kb, vb, nkb, nvb, ngb, sem, rsem, wsem,
+):
+    def start(src, dst, s):
+        cp = pltpu.make_async_copy(src, dst, s)
+        cp.start()
+        return cp
+
+    l_coef = start(coef, cv, sem.at[5])
+    reads = []
+    for b in range(FINISH):
+        rows = pl.ds(b * FROWS, FROWS)
+        reads.append(
+            (
+                start(dn.at[rows, :], dv.at[rows, :], rsem.at[b]),
+                start(act.at[rows, :], av.at[rows, :], rsem.at[FINISH + b]),
+            )
+        )
+    through = [
+        (start(src, mid, sem.at[i]), mid, dst)
+        for i, (src, mid, dst) in enumerate(
+            ((keys, kb, k_o), (values, vb, v_o), (nk, nkb, nk_o), (nv, nvb, nv_o), (ng, ngb, ng_o))
+        )
+    ]
+    passed = []
+    l_coef.wait()
+    for b in range(FINISH):
+        rows = pl.ds(b * FROWS, FROWS)
+        for cp in reads[b]:
+            cp.wait()
+        x = av[rows, :].astype(F32)
+        out[rows, :] = (dv[rows, :].astype(F32) - x * cv[rows, 0:1]).astype(BF16)
+        passed.append(start(out.at[rows, :], grad_o.at[rows, :], wsem.at[b]))
+        if b == FINISH // 2:
+            for i, (cp, mid, dst) in enumerate(through):
+                cp.wait()
+                passed.append(start(mid, dst, wsem.at[FINISH + i]))
+    for cp in passed:
+        cp.wait()
+
+
+def finish(act, dn, coef, keys, values, nk, nv, ng):
+    hbm = pl.BlockSpec(memory_space=pltpu.HBM)
+    shape = jax.ShapeDtypeStruct
+    DMA = pltpu.SemaphoreType.DMA
+    grad, k, v, nk, nv, ng = pl.pallas_call(
+        finish_kernel,
+        name="finish",
+        in_specs=[hbm] * 8,
+        out_specs=(hbm,) * 6,
+        out_shape=(
+            shape((512, 4096), BF16),
+            shape((512, 512), BF16),
+            shape((512, 512), BF16),
+            shape((1, 128, 512), F32),
+            shape((1, 128, 512), F32),
+            shape((1, 128), F32),
+        ),
+        scratch_shapes=[
+            pltpu.VMEM((512, 128), F32),
+            pltpu.VMEM((512, 4096), BF16),
+            pltpu.VMEM((512, 4096), BF16),
+            pltpu.VMEM((512, 4096), BF16),
+            pltpu.VMEM((512, 512), BF16),
+            pltpu.VMEM((512, 512), BF16),
+            pltpu.VMEM((1, 128, 512), F32),
+            pltpu.VMEM((1, 128, 512), F32),
+            pltpu.VMEM((1, 128), F32),
+            DMA((6,)),
+            DMA((2 * FINISH,)),
+            DMA((FINISH + 5,)),
+        ],
+        compiler_params=pltpu.CompilerParams(vmem_limit_bytes=60 << 20),
+        cost_estimate=pl.CostEstimate(
+            flops=3 * 512 * 4096, bytes_accessed=16 << 20, transcendentals=0
+        ),
+    )(act, dn, coef, keys, values, nk, nv, ng)
+    return k, v, grad, nk, nv, ng
 
 
 def solution(mesh):

time: 110 us -> 100 us (0.909)
  other arithmetic: 6.48 us -> 0 us
  local copies, waits for them, and re-layouts: 4.62 us -> 0 us
  Pallas kernels: 97.1 us -> 98.4 us
    convert_element_type x1 -> x0, other arithmetic: 6.48 us -> none  [body(): (dn.astype(F32) - activations.astype(F32) * coef[:, 0:1]).astype(BF16)]
    pallas_call x0 -> x1, Pallas kernels: none -> 6.12 us  [finish(): pl.pallas_call(finish_kernel, name='finish', in_specs=[hbm] * 8, out_spec...]
    pallas_call x1, Pallas kernels: 97.1 us -> 92.3 us  [body(): pl.pallas_call(kernel, name='group_step', out_shape=(shape((512, 512), BF...]
    unnamed x17 -> x0, local copies, waits for them, and re-layouts: 3.53 us -> none
where the time goes in v2:
time: 100 us; the launch traced here: 99.9 us
  Pallas kernels  98.4 us (98%)
  between operations  1.45 us (1%)
    pallas_call x1, Pallas kernels, body(): pl.pallas_call(kernel, name='group_step', out_shape=(shape((512, 512), BF...  92.3 us
    pallas_call x1, Pallas kernels, finish(): pl.pallas_call(finish_kernel, name='finish', in_specs=[hbm] * 8, out_spec...  6.12 us

profile of v2, /device:TPU:1, one launch (start us, length us, event | category | flops | bytes accessed | tf_op | source)
XLA Modules:
  0.0 99.9 jit_solution(1589085656326872147)
XLA Ops:
  1.3 92.3 %group_step.1 = (bf16[512,512]{1,0:T(8,128)(2,1)}, bf16[512,512]{1,0:T(8,128)(2,1)}, bf16[512,4096]{1,0:T(8,128)(2,1)}, f32[512,128]{1,0:T(8,128)}, f32[1,128,51...) custom-call(bf16[512,4096]{1,0:T(8,128)(2,1)} %act.3, f32[1,128]{1,0:T(1,128)} %gain_in.1, ...), custom_call_target="tpu_custom_call" | custom-call | flops 12999999488 | bytes 25165824 | tf_op jit(solution)/shard_map/group_step/pallas_call | solution.py:469
  93.6 6.1 %finish.1 = (bf16[512,4096]{1,0:T(8,128)(2,1)}, bf16[512,512]{1,0:T(8,128)(2,1)}, bf16[512,512]{1,0:T(8,128)(2,1)}, f32[1,128,512]{2,1,0:T(8,128)}, f32[1,128,512]{2,1,0:T(8,128)}, /*index=5*/f32[1,128]{1,0:T(1,128)}) custom-call(bf16[512,4096]{1,0:T(8,128)(2,1)} %act.3, bf16[512,4096]{1,0:T(8,128)(2,1)} %get-tuple-element.19.dn, ...), custom_call_target="tpu_custom_call" | custom-call | flops 6291456 | bytes 16777216 | tf_op jit(solution)/shard_map/finish/pallas_call | solution.py:590

commit v3 on v2

--- a/solution.py
+++ b/solution.py
@@ -343,6 +343,13 @@
             arrived(piece(dz, dx), agsem.at[dz * 4 + dx])
         send(piece(dz, dx), piece(dz, dx), sibsem.at[dz * 4 + dx], sibling)
 
+    def back(j, cols):
+        d = lax.dot_general(
+            ctv[...], gw[j], (((1,), (1,)), ((), ())), preferred_element_type=F32
+        )
+        dn_ref[:, cols] = (d * (inv_ref[:, 0:1] * (1.0 / 64.0))).astype(BF16)
+        pltpu.make_async_copy(dn_ref.at[:, cols], dn_out.at[:, cols], dsem).start()
+
     def pairs(first, items):
         for n, (dz, dx) in enumerate(items):
             arrived(sib_piece(dz, dx), sibsem.at[dz * 4 + dx])
@@ -350,20 +357,12 @@
             j = at(dz, dx)
             cols = pl.ds(pl.multiple_of(j * 256, 256), 256)
 
-            @pl.loop(0, 2)
-            def _(b):
-                rows = pl.ds(pl.multiple_of(b * 256, 256), 256)
-                part = jnp.dot(xv[rows, cols], gw[j], preferred_element_type=F32)
-                if first and n == 0:
-                    acc[rows, :] = part
-                else:
-                    acc[rows, :] += part
-                d = lax.dot_general(
-                    ctv[rows, :], gw[j], (((1,), (1,)), ((), ())), preferred_element_type=F32
-                )
-                dn_ref[rows, cols] = (d * (inv_ref[rows, 0:1] * (1.0 / 64.0))).astype(BF16)
-
-            pltpu.make_async_copy(dn_ref.at[:, cols], dn_out.at[:, cols], dsem).start()
+            back(j, cols)
+            part = jnp.dot(xv[:, cols], gw[j], preferred_element_type=F32)
+            if first and n == 0:
+                acc[...] = part
+            else:
+                acc[...] += part
 
     for r in range(ROUNDS):
         arrived(ctT.at[r, :, sib_lanes], ctsem.at[r])
@@ -417,26 +416,28 @@
     forward_left(3, 0, 128)
     swap_z(2)
     pairs(False, [(1, 3), (3, 1)])
-    swap_y(3)
     gathered(2, 3)
     forward_right(2, 0, 64)
     gathered(2, 1)
     forward_left(2, 64, 64)
-    swap_z(3)
     pairs(False, [(2, 3), (2, 1)])
     gathered(3, 3)
     gathered(1, 1)
     pairs(False, [(3, 3), (1, 1)])
+    swap_y(3)
     gathered(1, 2)
     gathered(3, 2)
     pairs(False, [(1, 2), (3, 2)])
     gathered(2, 2)
-    pairs(False, [(2, 2)])
+    arrived(sib_piece(2, 2), sibsem.at[10])
+    last = at(2, 2)
+    last_cols = pl.ds(pl.multiple_of(last * 256, 256), 256)
 
     for b in range(4):
         rows = pl.ds(b * 128, 128)
         inv = inv_ref[rows, 0:1]
-        kv = acc[rows, :] * (inv * (1.0 / 64.0))
+        part = jnp.dot(xv[rows, last_cols], gw[last], preferred_element_type=F32)
+        kv = (acc[rows, :] + part) * (inv * (1.0 / 64.0))
         inner = jnp.sum(kv * ctv[rows, :].astype(F32), axis=-1, keepdims=True) * (1.0 / 4096.0)
         keys_ref[rows, :] = kv[:, 0:512].astype(BF16)
         values_ref[rows, :] = kv[:, 512:1024].astype(BF16)
@@ -444,6 +445,8 @@
         out(keys_ref.at[rows, :], keys_out.at[rows, :])
         out(values_ref.at[rows, :], values_out.at[rows, :])
         out(coef_ref.at[rows, :], coef_out.at[rows, :])
+    back(last, last_cols)
+    swap_z(3)
 
     for cp in sends:
         cp.wait_send()

time: 100 us -> 96.4 us (0.964)
  Pallas kernels: 98.4 us -> 94.8 us
    pallas_call x1, Pallas kernels: 92.3 us -> 88.7 us  [body(): pl.pallas_call(kernel, name='group_step', out_shape=(shape((512, 512), BF...]
where the time goes in v3:
time: 96.4 us; the launch traced here: 96.3 us
  Pallas kernels  94.8 us (98%)
  between operations  1.45 us (2%)
    pallas_call x1, Pallas kernels, body(): pl.pallas_call(kernel, name='group_step', out_shape=(shape((512, 512), BF...  88.7 us
    pallas_call x1, Pallas kernels, finish(): pl.pallas_call(finish_kernel, name='finish', in_specs=[hbm] * 8, out_spec...  6.14 us

profile of v3, /device:TPU:1, one launch (start us, length us, event | category | flops | bytes accessed | tf_op | source)
XLA Modules:
  0.0 96.3 jit_solution(3125310889500005126)
XLA Ops:
  1.3 88.7 %group_step.1 = (bf16[512,512]{1,0:T(8,128)(2,1)}, bf16[512,512]{1,0:T(8,128)(2,1)}, bf16[512,4096]{1,0:T(8,128)(2,1)}, f32[512,128]{1,0:T(8,128)}, f32[1,128,51...) custom-call(bf16[512,4096]{1,0:T(8,128)(2,1)} %act.3, f32[1,128]{1,0:T(1,128)} %gain_in.1, ...), custom_call_target="tpu_custom_call" | custom-call | flops 12999999488 | bytes 25165824 | tf_op jit(solution)/shard_map/group_step/pallas_call | solution.py:472
  90.0 6.1 %finish.1 = (bf16[512,4096]{1,0:T(8,128)(2,1)}, bf16[512,512]{1,0:T(8,128)(2,1)}, bf16[512,512]{1,0:T(8,128)(2,1)}, f32[1,128,512]{2,1,0:T(8,128)}, f32[1,128,512]{2,1,0:T(8,128)}, /*index=5*/f32[1,128]{1,0:T(1,128)}) custom-call(bf16[512,4096]{1,0:T(8,128)(2,1)} %act.3, bf16[512,4096]{1,0:T(8,128)(2,1)} %get-tuple-element.19.dn, ...), custom_call_target="tpu_custom_call" | custom-call | flops 6291456 | bytes 16777216 | tf_op jit(solution)/shard_map/finish/pallas_call | solution.py:593

commit v4 on v3

--- a/solution.py
+++ b/solution.py
@@ -13,6 +13,7 @@
 lr_gain = 0.005
 
 FINISH = 8
+AHEAD = 8
 FROWS = 512 // FINISH
 NX = 4
 NZ = 4
@@ -206,15 +207,22 @@
         ms = jnp.sum(xb * xb, axis=-1, keepdims=True) * (1.0 / 4096.0)
         inv = lax.rsqrt(ms + 1e-05)
         inv_ref[rows, :] = jnp.broadcast_to(inv, (128, 128))
-        lanes = pl.ds(pl.multiple_of(c * 512 + b * 128, 128), 128)
-        for r in range(ROUNDS):
-            ct = ctv[rows, r * KR : (r + 1) * KR].astype(F32) * inv
-            ctT[r, :, lanes] = jnp.transpose(ct).astype(BF16)
 
     own_lanes = pl.ds(pl.multiple_of(c * 512, 512), 512)
     sib_lanes = pl.ds(pl.multiple_of(sib * 512, 512), 512)
-    for r in range(ROUNDS):
+
+    def turn(r):
+        @pl.loop(0, 4)
+        def _(b):
+            rows = pl.ds(pl.multiple_of(b * 128, 128), 128)
+            lanes = pl.ds(pl.multiple_of(c * 512 + b * 128, 128), 128)
+            ct = ctv[rows, r * KR : (r + 1) * KR].astype(F32) * inv_ref[rows, 0:1]
+            ctT[r, :, lanes] = jnp.transpose(ct).astype(BF16)
+
         send(ctT.at[r, :, own_lanes], ctT.at[r, :, own_lanes], ctsem.at[r], sibling)
+
+    turn(0)
+    turn(1)
     for cp in l_own:
         cp.wait()
 
@@ -364,17 +372,29 @@
             else:
                 acc[...] += part
 
-    for r in range(ROUNDS):
+    def turned(r):
         arrived(ctT.at[r, :, sib_lanes], ctsem.at[r])
-    for s in (2, 1, 3, 0):
-        arrived(x2h.at[s, sib_lanes, :], xsem.at[s])
+
+    def columns(t):
+        arrived(x2h.at[t, sib_lanes, :], xsem.at[t])
+
+    columns(2)
+    turned(0)
     send_opp(0)
+    columns(1)
+    columns(3)
     grad_block(0, 1)
     grad_block(0, 3)
     send_plain(0)
+    turned(1)
     send_opp(1)
+    turn(2)
+    turn(3)
     grad_block(1, 1)
     grad_block(1, 3)
+    columns(0)
+    turned(2)
+    turned(3)
     step(0)
     grad_block(0, 0)
     grad_block(1, 0)
@@ -394,6 +414,7 @@
     pairs(False, [(2, 0)])
     swap_y(0)
     step(3)
+    early = len(sends)
     forward_left(0, 64, 64)
     forward_right(0, 0, 64)
     for dr, dl in ((1, 3), (2, 2), (3, 1)):
@@ -425,6 +446,8 @@
     gathered(1, 1)
     pairs(False, [(3, 3), (1, 1)])
     swap_y(3)
+    for cp in sends[:early]:
+        cp.wait_send()
     gathered(1, 2)
     gathered(3, 2)
     pairs(False, [(1, 2), (3, 2)])
@@ -448,7 +471,7 @@
     back(last, last_cols)
     swap_z(3)
 
-    for cp in sends:
+    for cp in sends[early:]:
         cp.wait_send()
     for cp in outs:
         cp.wait()
@@ -555,7 +578,8 @@
 
     l_coef = start(coef, cv, sem.at[5])
     reads = []
-    for b in range(FINISH):
+
+    def read(b):
         rows = pl.ds(b * FROWS, FROWS)
         reads.append(
             (
@@ -570,9 +594,13 @@
         )
     ]
     passed = []
+    for b in range(AHEAD):
+        read(b)
     l_coef.wait()
     for b in range(FINISH):
         rows = pl.ds(b * FROWS, FROWS)
+        if b + AHEAD < FINISH:
+            read(b + AHEAD)
         for cp in reads[b]:
             cp.wait()
         x = av[rows, :].astype(F32)

time: 96.4 us -> 94.1 us (0.976)
  Pallas kernels: 94.8 us -> 92.6 us
    pallas_call x1, Pallas kernels: 88.7 us -> 86.4 us  [body(): pl.pallas_call(kernel, name='group_step', out_shape=(shape((512, 512), BF...]
where the time goes in v4:
time: 94.1 us; the launch traced here: 94 us
  Pallas kernels  92.6 us (98%)
  between operations  1.45 us (2%)
    pallas_call x1, Pallas kernels, body(): pl.pallas_call(kernel, name='group_step', out_shape=(shape((512, 512), BF...  86.4 us
    pallas_call x1, Pallas kernels, finish(): pl.pallas_call(finish_kernel, name='finish', in_specs=[hbm] * 8, out_spec...  6.14 us

profile of v4, /device:TPU:1, one launch (start us, length us, event | category | flops | bytes accessed | tf_op | source)
XLA Modules:
  0.0 94.0 jit_solution(5947283520613244642)
XLA Ops:
  1.3 86.4 %group_step.1 = (bf16[512,512]{1,0:T(8,128)(2,1)}, bf16[512,512]{1,0:T(8,128)(2,1)}, bf16[512,4096]{1,0:T(8,128)(2,1)}, f32[512,128]{1,0:T(8,128)}, f32[1,128,51...) custom-call(bf16[512,4096]{1,0:T(8,128)(2,1)} %act.3, f32[1,128]{1,0:T(1,128)} %gain_in.1, ...), custom_call_target="tpu_custom_call" | custom-call | flops 12999999488 | bytes 25165824 | tf_op jit(solution)/shard_map/group_step/pallas_call | solution.py:495
  87.7 6.1 %finish.1 = (bf16[512,4096]{1,0:T(8,128)(2,1)}, bf16[512,512]{1,0:T(8,128)(2,1)}, bf16[512,512]{1,0:T(8,128)(2,1)}, f32[1,128,512]{2,1,0:T(8,128)}, f32[1,128,512]{2,1,0:T(8,128)}, /*index=5*/f32[1,128]{1,0:T(1,128)}) custom-call(bf16[512,4096]{1,0:T(8,128)(2,1)} %act.3, bf16[512,4096]{1,0:T(8,128)(2,1)} %get-tuple-element.19.dn, ...), custom_call_target="tpu_custom_call" | custom-call | flops 6291456 | bytes 16777216 | tf_op jit(solution)/shard_map/finish/pallas_call | solution.py:621
